TPU v7x, 32 devices: a whole 2x2x4 slice. The times are simulated.
32 devices in a mesh: groups: 2 (over y), space: 4 (over z), dp: 2 (over x), chan: 2 (over core).
Axes of the slice: x: 2, y: 2, z: 4, core: 2. Of those that a mesh axis runs over, the one named last changes fastest.
Arguments:
- features: bfloat16 [4, 1024, 256], P(('groups', 'dp'), 'space'), parts along dimension 0, may hold values from -40 to 40
- neighbours: int32 [27, 2048], P(None, ('groups', 'space')), parts along dimension 1, may hold values from 0 to 384, as said below
- send_rows: int32 [32, 32], P(('groups', 'space')), parts along dimension 0, may hold values from 0 to 256, as said below
- noise_level: int32 [4], P(('groups', 'dp')), parts along dimension 0, may hold values from 0 to 999
- conv_weight: bfloat16 [27, 256, 256], P(None, None, 'chan'), may hold values from -0.078125 to 0.078125
- out_weight: bfloat16 [256, 256], P(None, 'chan'), may hold values from -0.375 to 0.375
- scale_table: float32 [1000, 256], P(None, 'chan'), may hold values from 0.1 to 1.9
- shift_table: float32 [1000, 256], P(None, 'chan'), may hold values from -3 to 3
- cotangent: bfloat16 [4, 1024, 256], P(('groups', 'dp'), 'space', 'chan'), parts along dimension 0, may hold values from -6 to 6
Outputs:
- mixed: bfloat16 [4, 1024, 256], P(('groups', 'dp'), 'space', 'chan'), parts along dimension 0
- grad_input: bfloat16 [4, 1024, 256], P(('groups', 'dp'), 'space', 'chan'), parts along dimension 0
- grad_weight: bfloat16 [54, 256, 256], P('groups', 'dp', 'chan'), parts along dimension 0
There are 2 independent parts, one for each index of `groups`. A program takes and returns all parts, laid end to end along the dimension named above; an argument that names none is the same for every part. Nothing has to cross between parts.
Inputs may be any that keep to these rules, and one draw needn't show every extreme that they name: neighbours[13, b] is the block's own row. Values below 256 are own rows; a value 256 + s * 32 + j is halo slot j from owner s and is always a filled slot; 384 means no neighbour. `send_rows`: row s * 4 + d holds in its first entries the rows that owner s sends to owner d, then 256 for unused slots; an owner sends nothing to itself; owners next to each other along space send 32 rows to each other, and in every draw some owner receives 32 rows from every other owner.
All inputs are finite; a program needn't handle non-finite values.
Results may differ from a plain program's by a relative error of at most 0.007.
Values may be sent and summed in bfloat16 or wider, within the bound.
A program may use at most 64 MiB of HBM per device.

v0:
```python
import math

import jax
import jax.numpy as jnp
from jax import lax
from jax.sharding import PartitionSpec as P

GS = 8


EPSILON = 1e-05


def on_device(
    features,
    neighbours,
    send_rows,
    noise_level,
    conv_weight,
    out_weight,
    scale_table,
    shift_table,
    cotangent,
):
    own_rows = features[0]
    row_count = own_rows.shape[0]
    channels = own_rows.shape[1]
    half_width = conv_weight.shape[2]
    core_index = lax.axis_index("chan")
    space_count = lax.axis_size("space")
    padded = jnp.concatenate([own_rows, jnp.zeros((1, channels), own_rows.dtype)], axis=0)
    targets = send_rows.reshape(-1)
    outgoing = padded[targets]
    arrived = lax.all_to_all(outgoing, "space", split_axis=0, concat_axis=0, tiled=True)
    halo_rows = arrived.shape[0]
    row_table = jnp.concatenate(
        [own_rows, arrived, jnp.zeros((1, channels), own_rows.dtype)], axis=0
    )
    gathered = row_table[neighbours]
    conv_out = jnp.einsum("ksc,kcd->sd", gathered, conv_weight, preferred_element_type=jnp.float32)
    group_count = half_width // GS
    entries = row_count * space_count * GS
    grouped = conv_out.reshape(row_count, group_count, GS)
    sum_first, sum_second = lax.psum(
        (jnp.sum(grouped, axis=(0, 2)), jnp.sum(grouped * grouped, axis=(0, 2))), "space"
    )
    group_mean = sum_first / entries
    group_var = sum_second / entries - group_mean * group_mean
    inv_std = lax.rsqrt(group_var + EPSILON)
    centred = (grouped - group_mean[None, :, None]) * inv_std[None, :, None]
    noise_row = noise_level[0]
    gain_row = lax.dynamic_index_in_dim(scale_table, noise_row, 0, keepdims=False)
    shift_row = lax.dynamic_index_in_dim(shift_table, noise_row, 0, keepdims=False)
    normed = centred.reshape(row_count, half_width) * gain_row[None, :] + shift_row[None, :]
    hidden = jax.nn.silu(normed).astype(jnp.bfloat16)
    hidden_full = lax.all_gather(hidden, "chan", axis=1, tiled=True)
    mixed_part = jnp.dot(hidden_full, out_weight, preferred_element_type=jnp.float32)
    residual_in = lax.dynamic_slice_in_dim(own_rows, core_index * half_width, half_width, 1).astype(
        jnp.float32
    )
    mixed = (residual_in + mixed_part).astype(jnp.bfloat16)[None]
    cot_rows = cotangent[0]
    cot_full, weight_full = (
        lax.all_gather(cot_rows, "chan", axis=1, tiled=True),
        lax.all_gather(out_weight, "chan", axis=1, tiled=True),
    )
    weight_rows = lax.dynamic_slice_in_dim(weight_full, core_index * half_width, half_width, 0)
    grad_hidden = lax.dot_general(
        cot_full, weight_rows, (((1,), (1,)), ((), ())), preferred_element_type=jnp.float32
    )
    sigmoid_val = jax.nn.sigmoid(normed)
    grad_normed = grad_hidden * sigmoid_val * (1.0 + normed * (1.0 - sigmoid_val))
    grad_centred = (grad_normed * gain_row[None, :]).reshape(row_count, group_count, GS)
    sum_grad, sum_cross = lax.psum(
        (jnp.sum(grad_centred, axis=(0, 2)), jnp.sum(grad_centred * centred, axis=(0, 2))), "space"
    )
    grad_conv = inv_std[None, :, None] * (
        grad_centred
        - sum_grad[None, :, None] / entries
        - centred * (sum_cross / entries)[None, :, None]
    )
    grad_conv = grad_conv.reshape(row_count, half_width).astype(jnp.bfloat16)
    partial_grad = jnp.einsum(
        "ksc,sd->kcd", gathered, grad_conv, preferred_element_type=jnp.float32
    )
    grad_scale = 1.0 / math.sqrt(lax.axis_size("dp") * row_count * space_count)
    total_grad = lax.psum(partial_grad, ("space", "dp"))
    share_rows = channels // lax.axis_size("dp")
    total_grad = lax.dynamic_slice_in_dim(
        total_grad, lax.axis_index("dp") * share_rows, share_rows, 1
    )
    grad_weight = (total_grad * grad_scale).astype(jnp.bfloat16)
    grad_rows = jnp.einsum(
        "sd,kcd->ksc", grad_conv, conv_weight, preferred_element_type=jnp.float32
    )
    grad_table = (
        jnp.zeros((row_count + halo_rows + 1, channels), jnp.float32).at[neighbours].add(grad_rows)
    )
    returned = lax.all_to_all(
        grad_table[row_count : row_count + halo_rows].astype(jnp.bfloat16),
        "space",
        split_axis=0,
        concat_axis=0,
        tiled=True,
    ).astype(jnp.float32)
    collected = jnp.zeros((row_count + 1, channels), jnp.float32).at[targets].add(returned)
    own_grad = lax.psum_scatter(
        (grad_table[:row_count] + collected[:row_count]).astype(jnp.bfloat16),
        "chan",
        scatter_dimension=1,
        tiled=True,
    ).astype(jnp.float32)
    grad_input = (own_grad + cot_rows.astype(jnp.float32)).astype(jnp.bfloat16)[None]
    return (mixed, grad_input, grad_weight)


def solution(mesh):
    in_specs = (
        P(("groups", "dp"), "space", None),
        P(None, ("groups", "space")),
        P(("groups", "space"), None),
        P(("groups", "dp")),
        P(None, None, "chan"),
        P(None, "chan"),
        P(None, "chan"),
        P(None, "chan"),
        P(("groups", "dp"), "space", "chan"),
    )
    out_specs = (
        P(("groups", "dp"), "space", "chan"),
        P(("groups", "dp"), "space", "chan"),
        P("groups", "dp", "chan"),
    )
    return jax.shard_map(
        on_device, mesh=mesh, in_specs=in_specs, out_specs=out_specs, check_vma=False
    )
```

profile of v0, /device:TPU:0, one launch (start us, length us, event | category | flops | bytes accessed | tf_op | source)
XLA Modules:
  0.0 273.6 jit_solution(15170803320930089749)
XLA Ops:
  8.0 0.9 reshape.68
  8.9 0.9 concatenate.6
  9.8 1.5 gather_fusion
  11.3 6.3 %all-to-all-start = ((bf16[4,32,256]{2,1,0:T(8,128)(2,1)}), bf16[4,32,256]{2,1,0:T(8,128)(2,1)S(1)}, u32[]{:S(2)}, u32[]{:S(2)}) async-start(bf16[4,32,256]{2,1,0:T(8,128)(2,1)} %bitcast.3), calls=%async_computation | async-start | bytes 131072 | tf_op jit(solution)/shard_map/all_to_all | solution.py:34
  18.3 0.8 compare_select_fusion
  19.1 2.2 all_gather.10
  21.2 2.1 all-gather
  23.4 0.7 fusion.17
  24.1 1.0 maximum_maximum_fusion
  25.1 20.0 %gather_fusion.1 = bf16[6912,256]{1,0:T(8,128)(2,1)} fusion(bf16[385,256]{1,0:T(8,128)(2,1)S(1)} %maximum_maximum_fusion, s32[7168]{0:T(1024)S(1)} %pad_clamp_fusion), kind=kCustom, calls=%fused_computation.1 | custom fusion | bytes 7105536 | tf_op jit(solution)/shard_map/gather | solution.py:39
  45.1 3.1 %fusion.21 = (f32[128]{0:T(128)S(1)}, f32[128]{0:T(128)S(1)}, f32[256,128]{1,0:T(8,128)S(1)}) fusion(bf16[27,256,256]{2,1,0:T(8,128)(2,1)} %bitcast.58, bf16[27,256,128]{2,1,0:T(8,128)(2,1)S(1)} %copy-done), kind=kOutput, calls=%fused_computation.50 | convolution fusion | flops 453082880 | bytes 5440512 | tf_op jit(solution)/shard_map/ksc,kcd->sd/dot_general | solution.py:40
  48.4 0.1 reduce_sum.51
  48.5 0.1 reduce_sum.54
  48.6 12.2 %all-reduce.2 = (f32[16]{0:T(128)S(1)}, f32[16]{0:T(128)S(1)}) all-reduce(f32[16]{0:T(128)S(1)} %reduce_sum.54, f32[16]{0:T(128)S(1)} %reduce_sum.51), channel_id=1, replica_groups=mesh['groups'=2,'space'=4,'dp'=2,'chan'=2] {'space'}, use_global_device_ids=true, to_apply=%region_5.6 | all-reduce | flops 32 | bytes 256 | tf_op jit(solution)/shard_map/psum | solution.py:44
  60.9 0.1 sub.39
  61.1 0.1 mul.92
  61.1 0.2 fusion.20
  61.5 0.1 reduce_sum.72
  61.7 0.1 reduce_sum.75
  61.8 8.4 %all-reduce.1 = (f32[16]{0:T(128)S(1)}, f32[16]{0:T(128)S(1)}) all-reduce(f32[16]{0:T(128)S(1)} %reduce_sum.75, f32[16]{0:T(128)S(1)} %reduce_sum.72), channel_id=1, replica_groups=mesh['groups'=2,'space'=4,'dp'=2,'chan'=2] {'space'}, use_global_device_ids=true, to_apply=%region_11.12 | all-reduce | flops 32 | bytes 256 | tf_op jit(solution)/shard_map/psum | solution.py:74
  70.6 4.0 %fusion.22 = f32[256,27,256]{2,0,1:T(8,128)} fusion(bf16[256,128,1]{1,0,2:T(8,128)(2,1)S(1)} %get-tuple-element.11, bf16[27,256,128]{2,1,0:T(8,128)(2,1)S(1)} %copy-done), kind=kOutput, calls=%fused_computation.51 | convolution fusion | flops 452984832 | bytes 8912896 | tf_op jit(solution)/shard_map/sd,kcd->ksc/dot_general | solution.py:93
  74.6 35.7 %scatter_custom_fusion = f32[385,256]{1,0:T(8,128)S(1)} fusion(s32[6912]{0:T(1024)S(1)} %reshape.81, f32[6912,256]{1,0:T(8,128)} %bitcast.60, f32[]{:T(128)} %constant.22.clone.1), kind=kCustom, calls=%fused_computation.16 | custom fusion | flops 1769472 | bytes 394752 | tf_op jit(solution)/shard_map/scatter-add | solution.py:97
  110.3 8.8 %all_to_all.21 = bf16[4,32,256]{2,1,0:T(8,128)(2,1)S(1)} all-to-all(bf16[4,32,256]{2,1,0:T(8,128)(2,1)S(1)} %bitcast.65), channel_id=1, replica_groups=mesh['groups'=2,'space'=4,'dp'=2,'chan'=2] {'space'}, dimensions={0} | all-to-all | bytes 131072 | tf_op jit(solution)/shard_map/all_to_all | solution.py:99
  119.2 1.4 scatter_custom_fusion.1
  120.6 0.8 copy.20
  121.4 5.0 %fusion.23 = f32[27,256,128]{2,1,0:T(8,128)} fusion(bf16[27,256,256]{2,1,0:T(8,128)(2,1)} %bitcast.59, bf16[256,128,1]{1,0,2:T(8,128)(2,1)S(1)} %get-tuple-element.11), kind=kOutput, calls=%fused_computation.52 | convolution fusion | flops 452984832 | bytes 7143424 | tf_op jit(solution)/shard_map/ksc,sd->kcd/dot_general | solution.py:83
  126.4 2.0 all_gather.9
  128.5 0.8 fusion.4
  129.3 0.9 copy.21
  130.2 0.7 fusion.14
  130.9 132.7 %all-reduce.5.cloned.1.call-done = f32[27,256,128]{2,1,0:T(8,128)} async-done(((f32[27,256,128]{2,1,0:T(8,128)}), f32[27,256,128]{2,1,0:T(8,128)}) %all-reduce.5.cloned.1.call-update) | async-done | bytes 3538960 | tf_op jit(solution)/shard_map/psum | solution.py:87
  263.5 2.6 multiply_convert_fusion
  (35 shorter events, 1.1 us)
Async XLA Ops:
  8.0 37.1 %copy-start = (bf16[27,256,128]{2,1,0:T(8,128)(2,1)S(1)}, bf16[27,256,128]{2,1,0:T(8,128)(2,1)}, u32[]{:S(2)}) copy-start(bf16[27,256,128]{2,1,0:T(8,128)(2,1)} %param.13) | copy-start | bytes 5308420
  11.3 12.8 %all-to-all-start = ((bf16[4,32,256]{2,1,0:T(8,128)(2,1)}), bf16[4,32,256]{2,1,0:T(8,128)(2,1)S(1)}, u32[]{:S(2)}, u32[]{:S(2)}) async-start(bf16[4,32,256]{2,1,0:T(8,128)(2,1)} %bitcast.3), calls=%async_computation | async-start | bytes 131072 | tf_op jit(solution)/shard_map/all_to_all | solution.py:34
  17.6 111.6 %reduce-scatter.4.cloned.1.call-start = ((), (), s32[]{:S(2)}) async-start(), calls=%async_computation.4 | async-start | bytes 196608
  121.4 142.2 %all-reduce.5.cloned.1.call-start = ((), (), s32[]{:S(2)}) async-start(), calls=%async_computation.3 | async-start | bytes 7077888 | tf_op jit(solution)/shard_map/psum | solution.py:87
  126.4 2.1 copy-start.1
  126.4 2.1 copy-start.2
  126.4 3.8 %copy-start.3 = (bf16[1,256,128]{2,1,0:T(8,128)(2,1)S(1)}, bf16[1,256,128]{2,1,0:T(8,128)(2,1)}, u32[]{:S(2)}) copy-start(bf16[1,256,128]{2,1,0:T(8,128)(2,1)} %param.17) | copy-start | bytes 196612
Sparse Core Ops, SparseCore 0:
  121.5 6.0 reduce-scatter.3
Sparse Core Ops, SparseCore 1:
  126.5 137.0 all-reduce.4
where the time goes:
time: 274 us
  waiting for transfers between devices  133 us (49%)
  other arithmetic  42.8 us (16%)
  blocking collectives  35.7 us (13%)
  local copies, waits for them, and re-layouts  26.7 us (10%)
  between operations  16.2 us (6%)
  matrix products  13.1 us (5%)
  starting transfers between devices  6.36 us (2%)
    psum x1, waiting for transfers between devices, on_device(): total_grad = lax.psum(partial_grad, ('space', 'dp'))  133 us
    scatter-add x1, other arithmetic, on_device(): jnp.zeros((row_count + halo_rows + 1, channels), jnp.float32).at[neighbours]  35.7 us
    gather x1, local copies, waits for them, and re-layouts, on_device(): gathered = row_table[neighbours]  20 us
    psum x1, blocking collectives, on_device(): lax.psum((jnp.sum(grouped, axis=(0, 2)), jnp.sum(grouped * grouped, axis=...  12.2 us
    all_to_all x1, blocking collectives, on_device(): lax.all_to_all(grad_table[row_count:row_count + halo_rows].astype(jnp.bfl...  8.84 us
    psum x1, blocking collectives, on_device(): lax.psum((jnp.sum(grad_centred, axis=(0, 2)), jnp.sum(grad_centred * cent...  8.37 us
    all_to_all x1, starting transfers between devices, on_device(): lax.all_to_all(outgoing, 'space', split_axis=0, concat_axis=0, tiled=True)  6.32 us
  transfers between devices with their start and end apart: 3, of which 1 were waited for; matrix products, arithmetic and copies ran while one was open for 3% of the time, Pallas kernels for 0%

commit v1 on v0

--- a/solution.py
+++ b/solution.py
@@ -1,8 +1,11 @@
+import functools
 import math
 
 import jax
 import jax.numpy as jnp
 from jax import lax
+from jax.experimental import pallas as pl
+from jax.experimental.pallas import tpu as pltpu
 from jax.sharding import PartitionSpec as P
 
 GS = 8
@@ -114,6 +117,449 @@
     return (mixed, grad_input, grad_weight)
 
 
+BF = jnp.bfloat16
+F32 = jnp.float32
+MESH = pl.DeviceIdType.MESH
+RESIDENT_SHARES = 8
+
+
+def nn(a, b):
+    return lax.dot_general(a, b, (((1,), (0,)), ((), ())), preferred_element_type=F32)
+
+
+def nt(a, b):
+    return lax.dot_general(a, b, (((1,), (1,)), ((), ())), preferred_element_type=F32)
+
+
+def tn(a, b):
+    return lax.dot_general(a, b, (((0,), (0,)), ((), ())), preferred_element_type=F32)
+
+
+def one_hot(index_row, first, count):
+    rows = lax.broadcasted_iota(jnp.int32, (count, index_row.shape[1]), 0) + first
+    return jnp.where(rows == index_row, 1.0, 0.0).astype(BF)
+
+
+def unit_kernel(
+    N,
+    Q,
+    feat_ref,
+    nb_ref,
+    sr_ref,
+    noise_ref,
+    w_ref,
+    ow_ref,
+    scale_ref,
+    shift_ref,
+    cot_ref,
+    mixed_ref,
+    gin_ref,
+    gw_ref,
+    feat_t,
+    tab,
+    tab_all,
+    nb_all,
+    r_own,
+    r_all,
+    out_rows,
+    halo_in,
+    gath,
+    wt,
+    gath_all,
+    cot_sib,
+    ow_sib,
+    st_own,
+    st_in,
+    hid_own,
+    hid_sib,
+    gc_own,
+    gc_all,
+    acc,
+    hg_own,
+    hg_in,
+    og,
+    og_send,
+    og_sib,
+    halo_s,
+    halo_r,
+    nb_s,
+    nb_r,
+    r_s,
+    r_r,
+    feat_s,
+    feat_r,
+    sib_s,
+    sib_r,
+    st_s,
+    st_r,
+    gc_s,
+    gc_r,
+    hg_s,
+    hg_r,
+):
+    S, C = feat_ref.shape
+    K = nb_ref.shape[0]
+    D = cot_ref.shape[1]
+    CAP = sr_ref.shape[1]
+    H = N * CAP
+    CQ = C // Q
+    G = D // GS
+    entries = S * N * GS
+    s = lax.axis_index("space")
+    p = lax.axis_index("dp")
+    c = lax.axis_index("chan")
+    sibling = {"chan": 1 - c}
+    zpeers = [lax.rem(s + i, N) for i in range(1, N)]
+    gpeers = []
+    for i in range(N):
+        for j in range(Q):
+            if i or j:
+                gpeers.append((lax.rem(s + i, N), lax.rem(p + j, Q)))
+    pending = []
+
+    def copy(src, dst, send, recv, where):
+        return pltpu.make_async_remote_copy(
+            src_ref=src, dst_ref=dst, send_sem=send, recv_sem=recv, device_id=where, device_id_type=MESH
+        )
+
+    def push(*args):
+        started = copy(*args)
+        started.start()
+        pending.append(started)
+
+    def rows(i, n):
+        return pl.ds(pl.multiple_of(i * n, n), n)
+
+    barrier = pltpu.get_barrier_semaphore()
+    pl.semaphore_signal(barrier, inc=1, device_id=sibling, device_id_type=MESH)
+    for d, q in gpeers:
+        pl.semaphore_signal(barrier, inc=1, device_id={"space": d, "dp": q}, device_id_type=MESH)
+
+    lane_h = lax.broadcasted_iota(jnp.int32, (1, H), 1)
+    spread = (
+        lax.broadcasted_iota(jnp.int32, (CAP, H), 1) % CAP
+        == lax.broadcasted_iota(jnp.int32, (CAP, H), 0)
+    ).astype(BF)
+    tiled = nn(sr_ref[...].astype(F32).astype(BF), spread)
+    keep = lax.broadcasted_iota(jnp.int32, (N, H), 1) // CAP == lax.broadcasted_iota(
+        jnp.int32, (N, H), 0
+    )
+    r_row = jnp.sum(jnp.where(keep, tiled, 0.0), axis=0, keepdims=True).astype(jnp.int32)
+    r_own[...] = jnp.broadcast_to(r_row, r_own.shape)
+    oh_send = one_hot(r_row, 0, S)
+    out_rows[...] = tn(oh_send, feat_ref[...]).astype(BF)
+    pl.semaphore_wait(barrier, len(gpeers) + 1)
+
+    for d in zpeers:
+        push(
+            out_rows.at[rows(d, CAP)], halo_in.at[rows(s, CAP)], halo_s.at[d], halo_r.at[s], {"space": d}
+        )
+    push(cot_ref, cot_sib, sib_s.at[0], sib_r.at[0], sibling)
+    push(ow_ref.at[rows(1 - c, D)], ow_sib, sib_s.at[1], sib_r.at[1], sibling)
+    feat_t[...] = feat_ref[...].T
+    for d in zpeers:
+        push(nb_ref, nb_all.at[s], nb_s.at[d], nb_r.at[s], {"space": d})
+        push(r_own, r_all.at[s], r_s.at[d], r_r.at[s], {"space": d})
+    for d, q in gpeers:
+        push(
+            feat_t.at[rows(q, CQ)],
+            tab_all.at[s, rows(p, CQ), pl.ds(0, S)],
+            feat_s.at[d * Q + q],
+            feat_r.at[s * Q + p],
+            {"space": d, "dp": q},
+        )
+    halo_in[rows(s, CAP), :] = jnp.zeros((CAP, C), BF)
+    hg_in[rows(s, CAP), :] = jnp.zeros((CAP, C), BF)
+    nb_all[s] = nb_ref[...]
+    r_all[s] = r_own[...]
+    tab_all[s, rows(p, CQ), pl.ds(0, S)] = feat_t[rows(p, CQ), :]
+    tab[:, pl.ds(0, S)] = feat_t[...]
+
+    def own_rows_step(k, carry):
+        gath[rows(k, C), :] = nn(feat_t[...], one_hot(nb_ref[pl.ds(k, 1), :], 0, S)).astype(BF)
+        wt[:, rows(k, C)] = w_ref[k].T
+        return carry
+
+    lax.fori_loop(0, K, own_rows_step, 0, unroll=3)
+
+    for d in zpeers:
+        copy(
+            out_rows.at[rows(d, CAP)], halo_in.at[rows(d, CAP)], halo_s.at[d], halo_r.at[d], {"space": d}
+        ).wait_recv()
+    halo_t = halo_in[...].T
+
+    def conv_step(k, total):
+        part = gath[rows(k, C), :] + nn(halo_t, one_hot(nb_ref[pl.ds(k, 1), :], S, H)).astype(BF)
+        gath[rows(k, C), :] = part
+        return total + nn(wt[:, rows(k, C)], part)
+
+    conv = lax.fori_loop(0, K, conv_step, jnp.zeros((D, S), F32), unroll=3)
+
+    def fold(v):
+        v = jnp.sum(v.reshape(G, GS, S), axis=1)
+        total = v[:, :128]
+        for i in range(1, S // 128):
+            total = total + v[:, i * 128 : (i + 1) * 128]
+        return total
+
+    member = (
+        lax.broadcasted_iota(jnp.int32, (D, G), 0) // GS == lax.broadcasted_iota(jnp.int32, (D, G), 1)
+    ).astype(F32)
+
+    def widen(v):
+        v = lax.dot_general(
+            member, v, (((1,), (0,)), ((), ())), precision=lax.Precision.HIGHEST, preferred_element_type=F32
+        )
+        return jnp.concatenate([v] * (S // 128), axis=1)
+
+    def send_sums(turn, first, second):
+        st_own[turn, 0] = fold(first)
+        st_own[turn, 1] = fold(second)
+        for d in zpeers:
+            push(
+                st_own.at[turn],
+                st_in.at[turn, s],
+                st_s.at[turn * N + d],
+                st_r.at[turn * N + s],
+                {"space": d},
+            )
+        st_in[turn, s] = st_own[turn]
+
+    def take_sums(turn):
+        for d in zpeers:
+            copy(
+                st_own.at[turn],
+                st_in.at[turn, d],
+                st_s.at[turn * N + d],
+                st_r.at[turn * N + d],
+                {"space": d},
+            ).wait_recv()
+        total = st_in[turn, 0]
+        for i in range(1, N):
+            total = total + st_in[turn, i]
+        total = jnp.sum(total, axis=2, keepdims=True)
+        return jnp.broadcast_to(total[0], (G, 128)), jnp.broadcast_to(total[1], (G, 128))
+
+    send_sums(0, conv, conv * conv)
+
+    def column(ref):
+        row = ref[pl.ds(noise_ref[0], 1), :]
+        col = jnp.broadcast_to(row, (128, D)).T
+        return jnp.concatenate([col] * (S // 128), axis=1)
+
+    gain = column(scale_ref)
+    shift = column(shift_ref)
+    copy(cot_ref, cot_sib, sib_s.at[0], sib_r.at[0], sibling).wait_recv()
+    copy(ow_ref.at[rows(1 - c, D)], ow_sib, sib_s.at[1], sib_r.at[1], sibling).wait_recv()
+    grad_hidden = nt(ow_ref[rows(c, D), :], cot_ref[...]) + nt(ow_sib[...], cot_sib[...])
+
+    sum_first, sum_second = take_sums(0)
+    mean = sum_first / entries
+    var = sum_second / entries - mean * mean
+    inv_std = widen(lax.rsqrt(var + EPSILON))
+    centred = (conv - widen(mean)) * inv_std
+    normed = centred * gain + shift
+    sig = 1.0 / (1.0 + jnp.exp(-normed))
+    hid_own[...] = (normed * sig).astype(BF)
+    push(hid_own, hid_sib, sib_s.at[2], sib_r.at[2], sibling)
+    grad_centred = grad_hidden * sig * (1.0 + normed * (1.0 - sig)) * gain
+    send_sums(1, grad_centred, grad_centred * centred)
+
+    copy(hid_own, hid_sib, sib_s.at[2], sib_r.at[2], sibling).wait_recv()
+    mixed_ref[...] = (
+        feat_ref[:, rows(c, D)].astype(F32)
+        + tn(hid_own[...], ow_ref[rows(c, D), :])
+        + tn(hid_sib[...], ow_ref[rows(1 - c, D), :])
+    ).astype(BF)
+
+    sum_grad, sum_cross = take_sums(1)
+    grad_conv = inv_std * (
+        grad_centred - widen(sum_grad / entries) - centred * widen(sum_cross / entries)
+    )
+    gc_own[...] = grad_conv.astype(BF)
+    for d, q in gpeers:
+        push(
+            gc_own,
+            gc_all.at[p, :, rows(s, S)],
+            gc_s.at[d * Q + q],
+            gc_r.at[s * Q + p],
+            {"space": d, "dp": q},
+        )
+    gc_all[p, :, rows(s, S)] = gc_own[...]
+
+    acc[...] = jnp.zeros_like(acc)
+
+    def table_step(k, carry):
+        hot = one_hot(nb_ref[pl.ds(k, 1), :], 0, S + H)
+        acc[...] += nn(w_ref[k], nt(gc_own[...], hot).astype(BF))
+        return carry
+
+    lax.fori_loop(0, K, table_step, 0, unroll=3)
+    hg_own[...] = acc[:, S:].T.astype(BF)
+    for d in zpeers:
+        push(hg_own.at[rows(d, CAP)], hg_in.at[rows(s, CAP)], hg_s.at[d], hg_r.at[s], {"space": d})
+
+    for d in zpeers:
+        copy(nb_ref, nb_all.at[d], nb_s.at[d], nb_r.at[d], {"space": d}).wait_recv()
+        copy(r_own, r_all.at[d], r_s.at[d], r_r.at[d], {"space": d}).wait_recv()
+    for d, q in gpeers:
+        copy(
+            feat_t.at[rows(q, CQ)],
+            tab_all.at[d, rows(q, CQ), pl.ds(0, S)],
+            feat_s.at[d * Q + q],
+            feat_r.at[d * Q + q],
+            {"space": d, "dp": q},
+        ).wait_recv()
+    for d in range(N):
+        total = jnp.zeros((C, H), F32)
+        for o in range(N):
+            line = r_all[o, 0:1, :]
+            move = (o - d) * CAP % H
+            if move:
+                line = jnp.concatenate([line[:, H - move :], line[:, : H - move]], axis=1)
+            line = jnp.where(lane_h // CAP == o, line, S)
+            total = total + nn(tab_all[o, :, pl.ds(0, S)], one_hot(line, 0, S))
+        tab_all[d, :, pl.ds(S, H)] = total.astype(BF)
+    for d in range(N):
+
+        def gather_step(k, carry, d=d):
+            part = nn(tab_all[d], one_hot(nb_all[d, pl.ds(k, 1), :], 0, S + H)).astype(BF)
+            for q in range(Q):
+                gath_all[q, rows(k, CQ), pl.ds(d * S, S)] = part[q * CQ : (q + 1) * CQ]
+            return carry
+
+        lax.fori_loop(0, K, gather_step, 0, unroll=3)
+
+    for d in zpeers:
+        copy(
+            hg_own.at[rows(d, CAP)], hg_in.at[rows(d, CAP)], hg_s.at[d], hg_r.at[d], {"space": d}
+        ).wait_recv()
+    og[...] = acc[:, :S].T + nn(one_hot(r_own[0:1, :], 0, S), hg_in[...])
+    og_send[...] = og[:, rows(1 - c, D)].astype(BF)
+    push(og_send, og_sib, sib_s.at[3], sib_r.at[3], sibling)
+
+    for d, q in gpeers:
+        copy(
+            gc_own,
+            gc_all.at[q, :, rows(d, S)],
+            gc_s.at[d * Q + q],
+            gc_r.at[d * Q + q],
+            {"space": d, "dp": q},
+        ).wait_recv()
+    scale = 1.0 / math.sqrt(Q * S * N)
+    batch = 3 if K % 3 == 0 else 1
+
+    def weight_step(k, carry):
+        here = rows(k, batch * CQ)
+        total = nt(gath_all[0, here, :], gc_all[0])
+        for q in range(1, Q):
+            total = total + nt(gath_all[q, here, :], gc_all[q])
+        gw_ref[here, :] = (total * scale).astype(BF)
+        return carry
+
+    lax.fori_loop(0, K // batch, weight_step, 0)
+
+    copy(og_send, og_sib, sib_s.at[3], sib_r.at[3], sibling).wait_recv()
+    gin_ref[...] = (
+        og[:, rows(c, D)].astype(BF).astype(F32)
+        + og_sib[...].astype(F32)
+        + cot_ref[...].astype(F32)
+    ).astype(BF)
+    for started in pending:
+        started.wait_send()
+
+
+def fused_on_device(
+    features,
+    neighbours,
+    send_rows,
+    noise_level,
+    conv_weight,
+    out_weight,
+    scale_table,
+    shift_table,
+    cotangent,
+):
+    N = lax.axis_size("space")
+    Q = lax.axis_size("dp")
+    S, C = features.shape[1:]
+    K, _, D = conv_weight.shape
+    CAP = send_rows.shape[1]
+    H = N * CAP
+    CQ = C // Q
+    G = D // GS
+    vmem = pl.BlockSpec(memory_space=pltpu.VMEM)
+    smem = pl.BlockSpec(memory_space=pltpu.SMEM)
+    dma = pltpu.SemaphoreType.DMA
+    mixed, grad_input, grad_weight = pl.pallas_call(
+        functools.partial(unit_kernel, N, Q),
+        out_shape=(
+            jax.ShapeDtypeStruct((S, D), BF),
+            jax.ShapeDtypeStruct((S, D), BF),
+            jax.ShapeDtypeStruct((K * CQ, D), BF),
+        ),
+        in_specs=[vmem, vmem, vmem, smem, vmem, vmem, vmem, vmem, vmem],
+        out_specs=(vmem, vmem, vmem),
+        scratch_shapes=[
+            pltpu.VMEM((C, S), BF),
+            pltpu.VMEM((C, S + H), BF),
+            pltpu.VMEM((N, C, S + H), BF),
+            pltpu.VMEM((N, K, S), jnp.int32),
+            pltpu.VMEM((8, H), jnp.int32),
+            pltpu.VMEM((N, 8, H), jnp.int32),
+            pltpu.VMEM((H, C), BF),
+            pltpu.VMEM((H, C), BF),
+            pltpu.VMEM((K * C, S), BF),
+            pltpu.VMEM((D, K * C), BF),
+            pltpu.VMEM((Q, K * CQ, N * S), BF),
+            pltpu.VMEM((S, D), BF),
+            pltpu.VMEM((D, D), BF),
+            pltpu.VMEM((2, 2, G, 128), F32),
+            pltpu.VMEM((2, N, 2, G, 128), F32),
+            pltpu.VMEM((D, S), BF),
+            pltpu.VMEM((D, S), BF),
+            pltpu.VMEM((D, S), BF),
+            pltpu.VMEM((Q, D, N * S), BF),
+            pltpu.VMEM((C, S + H), F32),
+            pltpu.VMEM((H, C), BF),
+            pltpu.VMEM((H, C), BF),
+            pltpu.VMEM((S, C), F32),
+            pltpu.VMEM((S, D), BF),
+            pltpu.VMEM((S, D), BF),
+            dma((N,)),
+            dma((N,)),
+            dma((N,)),
+            dma((N,)),
+            dma((N,)),
+            dma((N,)),
+            dma((N * Q,)),
+            dma((N * Q,)),
+            dma((4,)),
+            dma((4,)),
+            dma((2 * N,)),
+            dma((2 * N,)),
+            dma((N * Q,)),
+            dma((N * Q,)),
+            dma((N,)),
+            dma((N,)),
+        ],
+        compiler_params=pltpu.CompilerParams(
+            collective_id=0, has_side_effects=True, vmem_limit_bytes=52 * 1024 * 1024
+        ),
+    )(
+        features[0],
+        neighbours,
+        send_rows,
+        noise_level,
+        conv_weight,
+        out_weight,
+        scale_table,
+        shift_table,
+        cotangent[0],
+    )
+    return mixed[None], grad_input[None], grad_weight.reshape(K, CQ, D)
+
+
 def solution(mesh):
     in_specs = (
         P(("groups", "dp"), "space", None),
@@ -131,6 +577,8 @@
         P(("groups", "dp"), "space", "chan"),
         P("groups", "dp", "chan"),
     )
+    fits = mesh.shape["space"] * mesh.shape["dp"] <= RESIDENT_SHARES
+    per_device = fused_on_device if fits else on_device
     return jax.shard_map(
-        on_device, mesh=mesh, in_specs=in_specs, out_specs=out_specs, check_vma=False
-    )
+        per_device, mesh=mesh, in_specs=in_specs, out_specs=out_specs, check_vma=False
+    )

time: 274 us -> 71.9 us (0.26)
  waiting for transfers between devices: 133 us -> 0 us
  Pallas kernels: 0 us -> 60.6 us
  other arithmetic: 42.8 us -> 0 us
  blocking collectives: 35.7 us -> 0 us
  local copies, waits for them, and re-layouts: 26.7 us -> 9.52 us
  between operations: 16.2 us -> 1.3 us
  matrix products: 13.1 us -> 0 us
  starting transfers between devices: 6.36 us -> 0 us
    psum x1 -> x0, waiting for transfers between devices: 133 us -> none  [on_device(): total_grad = lax.psum(partial_grad, ('space', 'dp'))]
    pallas_call x0 -> x1, Pallas kernels: none -> 60.6 us  [fused_on_device(): pl.pallas_call(functools.partial(unit_kernel, N, Q), out_shape=(jax.Shape...]
    scatter-add x2 -> x0, other arithmetic: 37.1 us -> none  [the longest x1 35.7 us: on_device(): jnp.zeros((row_count + halo_rows + 1, channels), jnp.float32).at[neighbours]]
    gather x2 -> x0, local copies, waits for them, and re-layouts: 21.5 us -> none  [the longest x1 20 us: on_device(): gathered = row_table[neighbours]]
    psum x2 -> x0, blocking collectives: 20.6 us -> none  [the longest x1 12.2 us: on_device(): lax.psum((jnp.sum(grouped, axis=(0, 2)), jnp.sum(grouped * grouped, axis=...]
    dot_general x5 -> x0, matrix products: 13.1 us -> none  [the longest x1 4.95 us: on_device(): jnp.einsum('ksc,sd->kcd', gathered, grad_conv, preferred_element_type=jnp...]
    all_to_all x1 -> x0, blocking collectives: 8.84 us -> none  [on_device(): lax.all_to_all(grad_table[row_count:row_count + halo_rows].astype(jnp.bfl...]
    unnamed x10 -> x17, local copies, waits for them, and re-layouts: 1.73 us -> 9.52 us
  transfers between devices with their start and end apart: 3 -> 0, of which waited for: 1 -> 0; matrix products, arithmetic and copies ran while one was open for 3% -> 0% of each run, Pallas kernels for 0% -> 0%
where the time goes in v1:
time: 71.9 us; the launch traced here: 71.5 us
  Pallas kernels  60.6 us (84%)
  local copies, waits for them, and re-layouts  9.52 us (13%)
  between operations  1.3 us (2%)
    pallas_call x1, Pallas kernels, fused_on_device(): pl.pallas_call(functools.partial(unit_kernel, N, Q), out_shape=(jax.Shape...  60.6 us
    unnamed x17, local copies, waits for them, and re-layouts  9.52 us

profile of v1, /device:TPU:0, one launch (start us, length us, event | category | flops | bytes accessed | tf_op | source)
XLA Modules:
  0.0 71.5 jit_solution(15946578808371603024)
XLA Ops:
  1.3 0.0 copy-start
  1.3 1.0 %copy-done = f32[1000,128]{1,0:T(8,128)S(1)} copy-done((f32[1000,128]{1,0:T(8,128)S(1)}, f32[1000,128]{1,0:T(8,128)}, u32[]{:S(2)}) %copy-start) | copy-done | bytes 512024
  2.3 0.0 copy-start.1
  2.3 1.0 %copy-done.1 = f32[1000,128]{1,0:T(8,128)S(1)} copy-done((f32[1000,128]{1,0:T(8,128)S(1)}, f32[1000,128]{1,0:T(8,128)}, u32[]{:S(2)}) %copy-start.1) | copy-done | bytes 512024
  3.4 0.0 copy-start.2
  3.4 0.9 %copy-done.2 = bf16[1,256,256]{2,1,0:T(8,128)(2,1)S(1)} copy-done((bf16[1,256,256]{2,1,0:T(8,128)(2,1)S(1)}, bf16[1,256,256]{2,1,0:T(8,128)(2,1)}, u32[]{:S(2)}) %copy-start.2) | copy-done | bytes 131096
  4.3 0.0 copy-start.3
  4.3 0.8 %copy-done.3 = bf16[256,128]{1,0:T(8,128)(2,1)S(1)} copy-done((bf16[256,128]{1,0:T(8,128)(2,1)S(1)}, bf16[256,128]{1,0:T(8,128)(2,1)}, u32[]{:S(2)}) %copy-start.3) | copy-done | bytes 65560
  5.1 0.0 copy-start.4
  5.1 0.8 %copy-done.4 = bf16[1,256,128]{2,1,0:T(8,128)(2,1)S(1)} copy-done((bf16[1,256,128]{2,1,0:T(8,128)(2,1)S(1)}, bf16[1,256,128]{2,1,0:T(8,128)(2,1)}, u32[]{:S(2)}) %copy-start.4) | copy-done | bytes 65560
  5.9 0.0 copy-start.5
  5.9 0.8 %copy-done.5 = s32[27,256]{1,0:T(8,128)S(1)} copy-done((s32[27,256]{1,0:T(8,128)S(1)}, s32[27,256]{1,0:T(8,128)}, u32[]{:S(2)}) %copy-start.5) | copy-done | bytes 27672
  6.7 0.0 copy-start.6
  6.7 0.7 copy-done.6
  7.4 60.6 %shard_map.112 = (bf16[256,128]{1,0:T(8,128)(2,1)S(1)}, bf16[256,128]{1,0:T(8,128)(2,1)S(1)}, bf16[3456,128]{1,0:T(8,128)(2,1)}) custom-call(bf16[256,256]{1,0:T(8,128)(2,1)S(1)} %bitcast.5, s32[27,256]{1,0:T(8,128)S(1)} %copy-done.5, s32[4,32]{1,0:T(4,128)S(1)} %copy-done.6, s32[1]{0:T(128)S(6)} %copy.15.noise_ref, bf16[27,256,128]{2,1,0:T(8,128)(2,1)} %w_ref.1, ...), custom_call_target="tpu_custom_call" | custom-call | tf_op jit(solution)/shard_map/pallas_call | solution.py:494
  68.0 0.6 copy.16
  68.6 0.6 copy.17
  69.3 2.2 %copy.18 = bf16[27,128,128]{2,1,0:T(8,128)(2,1)} copy(bf16[27,128,128]{2,1,0:T(8,128)(2,1)} %bitcast.9) | data formatting | bytes 1769472
Async XLA Ops:
  1.3 1.0 %copy-start = (f32[1000,128]{1,0:T(8,128)S(1)}, f32[1000,128]{1,0:T(8,128)}, u32[]{:S(2)}) copy-start(f32[1000,128]{1,0:T(8,128)} %scale_ref.1) | copy-start | bytes 1536004
  2.3 1.0 %copy-start.1 = (f32[1000,128]{1,0:T(8,128)S(1)}, f32[1000,128]{1,0:T(8,128)}, u32[]{:S(2)}) copy-start(f32[1000,128]{1,0:T(8,128)} %shift_ref.1) | copy-start | bytes 1536004
  3.4 0.9 %copy-start.2 = (bf16[1,256,256]{2,1,0:T(8,128)(2,1)S(1)}, bf16[1,256,256]{2,1,0:T(8,128)(2,1)}, u32[]{:S(2)}) copy-start(bf16[1,256,256]{2,1,0:T(8,128)(2,1)} %param.9) | copy-start | bytes 393220
  4.3 0.8 %copy-start.3 = (bf16[256,128]{1,0:T(8,128)(2,1)S(1)}, bf16[256,128]{1,0:T(8,128)(2,1)}, u32[]{:S(2)}) copy-start(bf16[256,128]{1,0:T(8,128)(2,1)} %ow_ref.1) | copy-start | bytes 196612
  5.1 0.8 %copy-start.4 = (bf16[1,256,128]{2,1,0:T(8,128)(2,1)S(1)}, bf16[1,256,128]{2,1,0:T(8,128)(2,1)}, u32[]{:S(2)}) copy-start(bf16[1,256,128]{2,1,0:T(8,128)(2,1)} %param.17) | copy-start | bytes 196612
  5.9 0.8 %copy-start.5 = (s32[27,256]{1,0:T(8,128)S(1)}, s32[27,256]{1,0:T(8,128)}, u32[]{:S(2)}) copy-start(s32[27,256]{1,0:T(8,128)} %nb_ref.1) | copy-start | bytes 82948
  6.7 0.7 copy-start.6

commit v2 on v1

--- a/solution.py
+++ b/solution.py
@@ -136,27 +136,41 @@
 
 
 def one_hot(index_row, first, count):
-    rows = lax.broadcasted_iota(jnp.int32, (count, index_row.shape[1]), 0) + first
-    return jnp.where(rows == index_row, 1.0, 0.0).astype(BF)
+    pieces = []
+    for begin in range(first, first + count, 256):
+        size = min(256, first + count - begin)
+        rows = lax.broadcasted_iota(jnp.int32, (size, index_row.shape[1]), 0).astype(F32).astype(BF)
+        line = (index_row - begin).astype(F32).astype(BF)
+        hit = rows == jnp.broadcast_to(line, rows.shape)
+        pieces.append(jnp.where(hit, jnp.ones_like(rows), jnp.zeros_like(rows)))
+    return pieces[0] if len(pieces) == 1 else jnp.concatenate(pieces, axis=0)
 
 
 def unit_kernel(
     N,
     Q,
+    feat_hbm,
+    nb_hbm,
+    sr_hbm,
+    noise_ref,
+    w_hbm,
+    ow_hbm,
+    scale_hbm,
+    shift_hbm,
+    cot_hbm,
+    mixed_ref,
+    gin_ref,
+    gw_ref,
     feat_ref,
     nb_ref,
     sr_ref,
-    noise_ref,
     w_ref,
     ow_ref,
     scale_ref,
     shift_ref,
     cot_ref,
-    mixed_ref,
-    gin_ref,
-    gw_ref,
+    load_s,
     feat_t,
-    tab,
     tab_all,
     nb_all,
     r_own,
@@ -188,6 +202,8 @@
     r_r,
     feat_s,
     feat_r,
+    pass_s,
+    pass_r,
     sib_s,
     sib_r,
     st_s,
@@ -216,6 +232,7 @@
             if i or j:
                 gpeers.append((lax.rem(s + i, N), lax.rem(p + j, Q)))
     pending = []
+    batch = 3 if K % 3 == 0 else 1
 
     def copy(src, dst, send, recv, where):
         return pltpu.make_async_remote_copy(
@@ -230,10 +247,32 @@
     def rows(i, n):
         return pl.ds(pl.multiple_of(i * n, n), n)
 
+    def half(i, core):
+        return pl.ds(pl.multiple_of(i * CQ + core * (CQ // 2), CQ // 2), CQ // 2)
+
+    load = [
+        pltpu.make_async_copy(src, dst, load_s.at[i])
+        for i, (src, dst) in enumerate(
+            [
+                (sr_hbm, sr_ref),
+                (feat_hbm, feat_ref),
+                (ow_hbm, ow_ref),
+                (cot_hbm, cot_ref),
+                (nb_hbm, nb_ref),
+                (w_hbm, w_ref),
+                (scale_hbm, scale_ref),
+                (shift_hbm, shift_ref),
+            ]
+        )
+    ]
     barrier = pltpu.get_barrier_semaphore()
     pl.semaphore_signal(barrier, inc=1, device_id=sibling, device_id_type=MESH)
     for d, q in gpeers:
         pl.semaphore_signal(barrier, inc=1, device_id={"space": d, "dp": q}, device_id_type=MESH)
+    for one in load:
+        one.start()
+    for one in load[:2]:
+        one.wait()
 
     lane_h = lax.broadcasted_iota(jnp.int32, (1, H), 1)
     spread = (
@@ -248,6 +287,9 @@
     r_own[...] = jnp.broadcast_to(r_row, r_own.shape)
     oh_send = one_hot(r_row, 0, S)
     out_rows[...] = tn(oh_send, feat_ref[...]).astype(BF)
+    feat_t[...] = feat_ref[...].T
+    for one in load[2:5]:
+        one.wait()
     pl.semaphore_wait(barrier, len(gpeers) + 1)
 
     for d in zpeers:
@@ -256,14 +298,13 @@
         )
     push(cot_ref, cot_sib, sib_s.at[0], sib_r.at[0], sibling)
     push(ow_ref.at[rows(1 - c, D)], ow_sib, sib_s.at[1], sib_r.at[1], sibling)
-    feat_t[...] = feat_ref[...].T
     for d in zpeers:
         push(nb_ref, nb_all.at[s], nb_s.at[d], nb_r.at[s], {"space": d})
         push(r_own, r_all.at[s], r_s.at[d], r_r.at[s], {"space": d})
     for d, q in gpeers:
         push(
-            feat_t.at[rows(q, CQ)],
-            tab_all.at[s, rows(p, CQ), pl.ds(0, S)],
+            feat_t.at[half(q, c)],
+            tab_all.at[s, half(p, c), pl.ds(0, S)],
             feat_s.at[d * Q + q],
             feat_r.at[s * Q + p],
             {"space": d, "dp": q},
@@ -273,7 +314,7 @@
     nb_all[s] = nb_ref[...]
     r_all[s] = r_own[...]
     tab_all[s, rows(p, CQ), pl.ds(0, S)] = feat_t[rows(p, CQ), :]
-    tab[:, pl.ds(0, S)] = feat_t[...]
+    load[5].wait()
 
     def own_rows_step(k, carry):
         gath[rows(k, C), :] = nn(feat_t[...], one_hot(nb_ref[pl.ds(k, 1), :], 0, S)).astype(BF)
@@ -288,12 +329,14 @@
         ).wait_recv()
     halo_t = halo_in[...].T
 
-    def conv_step(k, total):
-        part = gath[rows(k, C), :] + nn(halo_t, one_hot(nb_ref[pl.ds(k, 1), :], S, H)).astype(BF)
-        gath[rows(k, C), :] = part
-        return total + nn(wt[:, rows(k, C)], part)
-
-    conv = lax.fori_loop(0, K, conv_step, jnp.zeros((D, S), F32), unroll=3)
+    def conv_step(j, total):
+        parts = []
+        for i in range(batch):
+            hot = one_hot(nb_ref[pl.ds(j * batch + i, 1), :], S, H)
+            parts.append(gath[rows(j * batch + i, C), :] + nn(halo_t, hot).astype(BF))
+        return total + nn(wt[:, rows(j, batch * C)], jnp.concatenate(parts, axis=0))
+
+    conv = lax.fori_loop(0, K // batch, conv_step, jnp.zeros((D, S), F32))
 
     def fold(v):
         v = jnp.sum(v.reshape(G, GS, S), axis=1)
@@ -347,11 +390,52 @@
         col = jnp.broadcast_to(row, (128, D)).T
         return jnp.concatenate([col] * (S // 128), axis=1)
 
+    load[6].wait()
+    load[7].wait()
     gain = column(scale_ref)
     shift = column(shift_ref)
     copy(cot_ref, cot_sib, sib_s.at[0], sib_r.at[0], sibling).wait_recv()
     copy(ow_ref.at[rows(1 - c, D)], ow_sib, sib_s.at[1], sib_r.at[1], sibling).wait_recv()
     grad_hidden = nt(ow_ref[rows(c, D), :], cot_ref[...]) + nt(ow_sib[...], cot_sib[...])
+
+    passed = []
+    for d in zpeers:
+        copy(nb_ref, nb_all.at[d], nb_s.at[d], nb_r.at[d], {"space": d}).wait_recv()
+        copy(r_own, r_all.at[d], r_s.at[d], r_r.at[d], {"space": d}).wait_recv()
+    for d, q in gpeers:
+        mine = tab_all.at[d, half(q, c), pl.ds(0, S)]
+        other = tab_all.at[d, half(q, 1 - c), pl.ds(0, S)]
+        slot = d * Q + q
+        copy(
+            feat_t.at[half(q, c)], mine, feat_s.at[slot], feat_r.at[slot], {"space": d, "dp": q}
+        ).wait_recv()
+        push(mine, mine, pass_s.at[slot], pass_r.at[slot], sibling)
+        passed.append(copy(other, other, pass_s.at[slot], pass_r.at[slot], sibling))
+    for one in passed:
+        one.wait_recv()
+    for d in range(N):
+        total = jnp.zeros((C, H), F32)
+        for o in range(N):
+            line = r_all[o, 0:1, :]
+            move = (o - d) * CAP % H
+            if move:
+                line = jnp.concatenate([line[:, H - move :], line[:, : H - move]], axis=1)
+            line = jnp.where(lane_h // CAP == o, line, S)
+            total = total + nn(tab_all[o, :, pl.ds(0, S)], one_hot(line, 0, S))
+        tab_all[d, :, pl.ds(S, H)] = total.astype(BF)
+
+    def gather_rows(owners):
+        def gather_step(k, carry):
+            for d in owners:
+                hot = one_hot(nb_all[d, pl.ds(k, 1), :], 0, S + H)
+                part = nn(tab_all[d], hot).astype(BF)
+                for q in range(Q):
+                    gath_all[q, rows(k, CQ), pl.ds(d * S, S)] = part[q * CQ : (q + 1) * CQ]
+            return carry
+
+        lax.fori_loop(0, K, gather_step, 0, unroll=3)
+
+    gather_rows(range(N // 2))
 
     sum_first, sum_second = take_sums(0)
     mean = sum_first / entries
@@ -372,73 +456,20 @@
         + tn(hid_sib[...], ow_ref[rows(1 - c, D), :])
     ).astype(BF)
 
+    gather_rows(range(N // 2, N))
+
     sum_grad, sum_cross = take_sums(1)
     grad_conv = inv_std * (
         grad_centred - widen(sum_grad / entries) - centred * widen(sum_cross / entries)
     )
     gc_own[...] = grad_conv.astype(BF)
-    for d, q in gpeers:
-        push(
-            gc_own,
-            gc_all.at[p, :, rows(s, S)],
-            gc_s.at[d * Q + q],
-            gc_r.at[s * Q + p],
-            {"space": d, "dp": q},
-        )
-    gc_all[p, :, rows(s, S)] = gc_own[...]
-
-    acc[...] = jnp.zeros_like(acc)
-
-    def table_step(k, carry):
-        hot = one_hot(nb_ref[pl.ds(k, 1), :], 0, S + H)
-        acc[...] += nn(w_ref[k], nt(gc_own[...], hot).astype(BF))
-        return carry
-
-    lax.fori_loop(0, K, table_step, 0, unroll=3)
-    hg_own[...] = acc[:, S:].T.astype(BF)
-    for d in zpeers:
-        push(hg_own.at[rows(d, CAP)], hg_in.at[rows(s, CAP)], hg_s.at[d], hg_r.at[s], {"space": d})
-
-    for d in zpeers:
-        copy(nb_ref, nb_all.at[d], nb_s.at[d], nb_r.at[d], {"space": d}).wait_recv()
-        copy(r_own, r_all.at[d], r_s.at[d], r_r.at[d], {"space": d}).wait_recv()
-    for d, q in gpeers:
-        copy(
-            feat_t.at[rows(q, CQ)],
-            tab_all.at[d, rows(q, CQ), pl.ds(0, S)],
-            feat_s.at[d * Q + q],
-            feat_r.at[d * Q + q],
-            {"space": d, "dp": q},
-        ).wait_recv()
-    for d in range(N):
-        total = jnp.zeros((C, H), F32)
-        for o in range(N):
-            line = r_all[o, 0:1, :]
-            move = (o - d) * CAP % H
-            if move:
-                line = jnp.concatenate([line[:, H - move :], line[:, : H - move]], axis=1)
-            line = jnp.where(lane_h // CAP == o, line, S)
-            total = total + nn(tab_all[o, :, pl.ds(0, S)], one_hot(line, 0, S))
-        tab_all[d, :, pl.ds(S, H)] = total.astype(BF)
-    for d in range(N):
-
-        def gather_step(k, carry, d=d):
-            part = nn(tab_all[d], one_hot(nb_all[d, pl.ds(k, 1), :], 0, S + H)).astype(BF)
-            for q in range(Q):
-                gath_all[q, rows(k, CQ), pl.ds(d * S, S)] = part[q * CQ : (q + 1) * CQ]
-            return carry
-
-        lax.fori_loop(0, K, gather_step, 0, unroll=3)
-
-    for d in zpeers:
-        copy(
-            hg_own.at[rows(d, CAP)], hg_in.at[rows(d, CAP)], hg_s.at[d], hg_r.at[d], {"space": d}
-        ).wait_recv()
-    og[...] = acc[:, :S].T + nn(one_hot(r_own[0:1, :], 0, S), hg_in[...])
-    og_send[...] = og[:, rows(1 - c, D)].astype(BF)
-    push(og_send, og_sib, sib_s.at[3], sib_r.at[3], sibling)
-
-    for d, q in gpeers:
+    def pass_over_dp(d, src):
+        for q in [lax.rem(p + j, Q) for j in range(1, Q)]:
+            push(
+                src, gc_all.at[p, :, rows(d, S)], gc_s.at[d * Q + q], gc_r.at[d * Q + p], {"dp": q}
+            )
+
+    def gc_arrived(d, q):
         copy(
             gc_own,
             gc_all.at[q, :, rows(d, S)],
@@ -446,8 +477,47 @@
             gc_r.at[d * Q + q],
             {"space": d, "dp": q},
         ).wait_recv()
+
+    for d in zpeers:
+        push(gc_own, gc_all.at[p, :, rows(s, S)], gc_s.at[d * Q + p], gc_r.at[s * Q + p], {"space": d})
+    pass_over_dp(s, gc_own)
+    gc_all[p, :, rows(s, S)] = gc_own[...]
+
+    acc[...] = jnp.zeros_like(acc)
+
+    gc_rows = gc_own[...].T
+
+    def table_step(j, carry):
+        sums, weights = [], []
+        for i in range(batch):
+            hot = one_hot(nb_ref[pl.ds(j * batch + i, 1), :], 0, S + H)
+            sums.append(nn(hot, gc_rows).astype(BF))
+            weights.append(w_ref[j * batch + i])
+        acc[...] += nt(jnp.concatenate(sums, axis=1), jnp.concatenate(weights, axis=1))
+        return carry
+
+    steps = K // batch
+    early = steps * 5 // 9
+    lax.fori_loop(0, early, table_step, 0)
+    for d in zpeers:
+        gc_arrived(d, p)
+        pass_over_dp(d, gc_all.at[p, :, rows(d, S)])
+    lax.fori_loop(early, steps, table_step, 0)
+    hg_own[...] = acc[S:, :].astype(BF)
+    for d in zpeers:
+        push(hg_own.at[rows(d, CAP)], hg_in.at[rows(s, CAP)], hg_s.at[d], hg_r.at[s], {"space": d})
+
+    for d in zpeers:
+        copy(
+            hg_own.at[rows(d, CAP)], hg_in.at[rows(d, CAP)], hg_s.at[d], hg_r.at[d], {"space": d}
+        ).wait_recv()
+    og[...] = acc[:S, :] + nn(one_hot(r_own[0:1, :], 0, S), hg_in[...])
+    og_send[...] = og[:, rows(1 - c, D)].astype(BF)
+    push(og_send, og_sib, sib_s.at[3], sib_r.at[3], sibling)
+
+    for d, q in [(lax.rem(s + i, N), lax.rem(p + j, Q)) for i in range(N) for j in range(1, Q)]:
+        gc_arrived(d, q)
     scale = 1.0 / math.sqrt(Q * S * N)
-    batch = 3 if K % 3 == 0 else 1
 
     def weight_step(k, carry):
         here = rows(k, batch * CQ)
@@ -489,6 +559,7 @@
     CQ = C // Q
     G = D // GS
     vmem = pl.BlockSpec(memory_space=pltpu.VMEM)
+    hbm = pl.BlockSpec(memory_space=pltpu.HBM)
     smem = pl.BlockSpec(memory_space=pltpu.SMEM)
     dma = pltpu.SemaphoreType.DMA
     mixed, grad_input, grad_weight = pl.pallas_call(
@@ -498,11 +569,19 @@
             jax.ShapeDtypeStruct((S, D), BF),
             jax.ShapeDtypeStruct((K * CQ, D), BF),
         ),
-        in_specs=[vmem, vmem, vmem, smem, vmem, vmem, vmem, vmem, vmem],
+        in_specs=[hbm, hbm, hbm, smem, hbm, hbm, hbm, hbm, hbm],
         out_specs=(vmem, vmem, vmem),
         scratch_shapes=[
+            pltpu.VMEM((S, C), BF),
+            pltpu.VMEM((K, S), jnp.int32),
+            pltpu.VMEM((N, CAP), jnp.int32),
+            pltpu.VMEM((K, C, D), BF),
+            pltpu.VMEM((C, D), BF),
+            pltpu.VMEM(scale_table.shape, F32),
+            pltpu.VMEM(scale_table.shape, F32),
+            pltpu.VMEM((S, D), BF),
+            dma((8,)),
             pltpu.VMEM((C, S), BF),
-            pltpu.VMEM((C, S + H), BF),
             pltpu.VMEM((N, C, S + H), BF),
             pltpu.VMEM((N, K, S), jnp.int32),
             pltpu.VMEM((8, H), jnp.int32),
@@ -520,7 +599,7 @@
             pltpu.VMEM((D, S), BF),
             pltpu.VMEM((D, S), BF),
             pltpu.VMEM((Q, D, N * S), BF),
-            pltpu.VMEM((C, S + H), F32),
+            pltpu.VMEM((S + H, C), F32),
             pltpu.VMEM((H, C), BF),
             pltpu.VMEM((H, C), BF),
             pltpu.VMEM((S, C), F32),
@@ -532,6 +611,8 @@
             dma((N,)),
             dma((N,)),
             dma((N,)),
+            dma((N * Q,)),
+            dma((N * Q,)),
             dma((N * Q,)),
             dma((N * Q,)),
             dma((4,)),
@@ -544,7 +625,7 @@
             dma((N,)),
         ],
         compiler_params=pltpu.CompilerParams(
-            collective_id=0, has_side_effects=True, vmem_limit_bytes=52 * 1024 * 1024
+            collective_id=0, has_side_effects=True, vmem_limit_bytes=60 * 1024 * 1024
         ),
     )(
         features[0],

time: 71.9 us -> 58.9 us (0.82)
  Pallas kernels: 60.6 us -> 52.2 us
  local copies, waits for them, and re-layouts: 9.52 us -> 5.12 us
    pallas_call x1, Pallas kernels: 60.6 us -> 52.2 us  [fused_on_device(): pl.pallas_call(functools.partial(unit_kernel, N, Q), out_shape=(jax.Shape...]
    unnamed x17 -> x3, local copies, waits for them, and re-layouts: 9.52 us -> 5.12 us
where the time goes in v2:
time: 58.9 us; the launch traced here: 58.6 us
  Pallas kernels  52.2 us (89%)
  local copies, waits for them, and re-layouts  5.12 us (9%)
  between operations  1.29 us (2%)
    pallas_call x1, Pallas kernels, fused_on_device(): pl.pallas_call(functools.partial(unit_kernel, N, Q), out_shape=(jax.Shape...  52.2 us
    unnamed x3, local copies, waits for them, and re-layouts  5.12 us

profile of v2, /device:TPU:0, one launch (start us, length us, event | category | flops | bytes accessed | tf_op | source)
XLA Modules:
  0.0 58.6 jit_solution(18414422149501901887)
XLA Ops:
  1.3 52.2 %shard_map.112 = (bf16[256,128]{1,0:T(8,128)(2,1)}, bf16[256,128]{1,0:T(8,128)(2,1)}, bf16[3456,128]{1,0:T(8,128)(2,1)}) custom-call(bf16[256,256]{1,0:T(8,128)(2,1)} %bitcast.6, s32[27,256]{1,0:T(8,128)} %nb_hbm.1, s32[4,32]{1,0:T(4,128)} %sr_hbm.1, s32[1]{0:T(128)S(6)} %copy.15.noise_ref, bf16[27,256,128]{2,1,0:T(8,128)(2,1)} %w_hbm.1, ...), custom_call_target="tpu_custom_call" | custom-call | tf_op jit(solution)/shard_map/pallas_call | solution.py:565
  53.5 1.5 %copy.16 = bf16[1,256,128]{2,1,0:T(8,128)(2,1)} copy(bf16[1,256,128]{2,1,0:T(8,128)(2,1)} %bitcast.9) | data formatting | bytes 131072
  55.0 1.5 %copy.17 = bf16[1,256,128]{2,1,0:T(8,128)(2,1)} copy(bf16[1,256,128]{2,1,0:T(8,128)(2,1)} %bitcast.8) | data formatting | bytes 131072
  56.4 2.2 %copy.18 = bf16[27,128,128]{2,1,0:T(8,128)(2,1)} copy(bf16[27,128,128]{2,1,0:T(8,128)(2,1)} %bitcast.5) | data formatting | bytes 1769472

commit v3 on v2

--- a/solution.py
+++ b/solution.py
@@ -411,6 +411,26 @@
         ).wait_recv()
         push(mine, mine, pass_s.at[slot], pass_r.at[slot], sibling)
         passed.append(copy(other, other, pass_s.at[slot], pass_r.at[slot], sibling))
+
+    sum_first, sum_second = take_sums(0)
+    mean = sum_first / entries
+    var = sum_second / entries - mean * mean
+    inv_std = widen(lax.rsqrt(var + EPSILON))
+    centred = (conv - widen(mean)) * inv_std
+    normed = centred * gain + shift
+    sig = 1.0 / (1.0 + jnp.exp(-normed))
+    hid_own[...] = (normed * sig).astype(BF)
+    push(hid_own, hid_sib, sib_s.at[2], sib_r.at[2], sibling)
+    grad_centred = grad_hidden * sig * (1.0 + normed * (1.0 - sig)) * gain
+    send_sums(1, grad_centred, grad_centred * centred)
+
+    copy(hid_own, hid_sib, sib_s.at[2], sib_r.at[2], sibling).wait_recv()
+    mixed_ref[...] = (
+        feat_ref[:, rows(c, D)].astype(F32)
+        + tn(hid_own[...], ow_ref[rows(c, D), :])
+        + tn(hid_sib[...], ow_ref[rows(1 - c, D), :])
+    ).astype(BF)
+
     for one in passed:
         one.wait_recv()
     for d in range(N):
@@ -435,28 +455,7 @@
 
         lax.fori_loop(0, K, gather_step, 0, unroll=3)
 
-    gather_rows(range(N // 2))
-
-    sum_first, sum_second = take_sums(0)
-    mean = sum_first / entries
-    var = sum_second / entries - mean * mean
-    inv_std = widen(lax.rsqrt(var + EPSILON))
-    centred = (conv - widen(mean)) * inv_std
-    normed = centred * gain + shift
-    sig = 1.0 / (1.0 + jnp.exp(-normed))
-    hid_own[...] = (normed * sig).astype(BF)
-    push(hid_own, hid_sib, sib_s.at[2], sib_r.at[2], sibling)
-    grad_centred = grad_hidden * sig * (1.0 + normed * (1.0 - sig)) * gain
-    send_sums(1, grad_centred, grad_centred * centred)
-
-    copy(hid_own, hid_sib, sib_s.at[2], sib_r.at[2], sibling).wait_recv()
-    mixed_ref[...] = (
-        feat_ref[:, rows(c, D)].astype(F32)
-        + tn(hid_own[...], ow_ref[rows(c, D), :])
-        + tn(hid_sib[...], ow_ref[rows(1 - c, D), :])
-    ).astype(BF)
-
-    gather_rows(range(N // 2, N))
+    gather_rows(range(1))
 
     sum_grad, sum_cross = take_sums(1)
     grad_conv = inv_std * (
@@ -499,6 +498,7 @@
     steps = K // batch
     early = steps * 5 // 9
     lax.fori_loop(0, early, table_step, 0)
+    gather_rows(range(1, 2))
     for d in zpeers:
         gc_arrived(d, p)
         pass_over_dp(d, gc_all.at[p, :, rows(d, S)])
@@ -506,6 +506,7 @@
     hg_own[...] = acc[S:, :].astype(BF)
     for d in zpeers:
         push(hg_own.at[rows(d, CAP)], hg_in.at[rows(s, CAP)], hg_s.at[d], hg_r.at[s], {"space": d})
+    gather_rows(range(2, N))
 
     for d in zpeers:
         copy(

time: 58.9 us -> 52.3 us (0.89)
  Pallas kernels: 52.2 us -> 45.1 us
    pallas_call x1, Pallas kernels: 52.2 us -> 45.1 us  [fused_on_device(): pl.pallas_call(functools.partial(unit_kernel, N, Q), out_shape=(jax.Shape...]
where the time goes in v3:
time: 52.3 us; the launch traced here: 51.5 us
  Pallas kernels  45.1 us (86%)
  local copies, waits for them, and re-layouts  5.12 us (10%)
  between operations  1.29 us (2%)
    pallas_call x1, Pallas kernels, fused_on_device(): pl.pallas_call(functools.partial(unit_kernel, N, Q), out_shape=(jax.Shape...  45.1 us
    unnamed x3, local copies, waits for them, and re-layouts  5.12 us

profile of v3, /device:TPU:0, one launch (start us, length us, event | category | flops | bytes accessed | tf_op | source)
XLA Modules:
  0.0 51.5 jit_solution(10551370928305264854)
XLA Ops:
  1.3 45.1 %shard_map.112 = (bf16[256,128]{1,0:T(8,128)(2,1)}, bf16[256,128]{1,0:T(8,128)(2,1)}, bf16[3456,128]{1,0:T(8,128)(2,1)}) custom-call(bf16[256,256]{1,0:T(8,128)(2,1)} %bitcast.6, s32[27,256]{1,0:T(8,128)} %nb_hbm.1, s32[4,32]{1,0:T(4,128)} %sr_hbm.1, s32[1]{0:T(128)S(6)} %copy.15.noise_ref, bf16[27,256,128]{2,1,0:T(8,128)(2,1)} %w_hbm.1, ...), custom_call_target="tpu_custom_call" | custom-call | tf_op jit(solution)/shard_map/pallas_call | solution.py:566
  46.4 1.5 %copy.16 = bf16[1,256,128]{2,1,0:T(8,128)(2,1)} copy(bf16[1,256,128]{2,1,0:T(8,128)(2,1)} %bitcast.9) | data formatting | bytes 131072
  47.9 1.5 %copy.17 = bf16[1,256,128]{2,1,0:T(8,128)(2,1)} copy(bf16[1,256,128]{2,1,0:T(8,128)(2,1)} %bitcast.8) | data formatting | bytes 131072
  49.4 2.2 %copy.18 = bf16[27,128,128]{2,1,0:T(8,128)(2,1)} copy(bf16[27,128,128]{2,1,0:T(8,128)(2,1)} %bitcast.5) | data formatting | bytes 1769472

commit v4 on v3

--- a/solution.py
+++ b/solution.py
@@ -321,7 +321,7 @@
         wt[:, rows(k, C)] = w_ref[k].T
         return carry
 
-    lax.fori_loop(0, K, own_rows_step, 0, unroll=3)
+    lax.fori_loop(0, K, own_rows_step, 0, unroll=9)
 
     for d in zpeers:
         copy(
@@ -336,7 +336,7 @@
             parts.append(gath[rows(j * batch + i, C), :] + nn(halo_t, hot).astype(BF))
         return total + nn(wt[:, rows(j, batch * C)], jnp.concatenate(parts, axis=0))
 
-    conv = lax.fori_loop(0, K // batch, conv_step, jnp.zeros((D, S), F32))
+    conv = lax.fori_loop(0, K // batch, conv_step, jnp.zeros((D, S), F32), unroll=3)
 
     def fold(v):
         v = jnp.sum(v.reshape(G, GS, S), axis=1)
@@ -453,7 +453,7 @@
                     gath_all[q, rows(k, CQ), pl.ds(d * S, S)] = part[q * CQ : (q + 1) * CQ]
             return carry
 
-        lax.fori_loop(0, K, gather_step, 0, unroll=3)
+        lax.fori_loop(0, K, gather_step, 0, unroll=9 // len(owners))
 
     gather_rows(range(1))
 
@@ -497,12 +497,12 @@
 
     steps = K // batch
     early = steps * 5 // 9
-    lax.fori_loop(0, early, table_step, 0)
+    lax.fori_loop(0, early, table_step, 0, unroll=2)
     gather_rows(range(1, 2))
     for d in zpeers:
         gc_arrived(d, p)
         pass_over_dp(d, gc_all.at[p, :, rows(d, S)])
-    lax.fori_loop(early, steps, table_step, 0)
+    lax.fori_loop(early, steps, table_step, 0, unroll=2)
     hg_own[...] = acc[S:, :].astype(BF)
     for d in zpeers:
         push(hg_own.at[rows(d, CAP)], hg_in.at[rows(s, CAP)], hg_s.at[d], hg_r.at[s], {"space": d})
@@ -528,7 +528,7 @@
         gw_ref[here, :] = (total * scale).astype(BF)
         return carry
 
-    lax.fori_loop(0, K // batch, weight_step, 0)
+    lax.fori_loop(0, K // batch, weight_step, 0, unroll=3)
 
     copy(og_send, og_sib, sib_s.at[3], sib_r.at[3], sibling).wait_recv()
     gin_ref[...] = (

time: 52.3 us -> 50.2 us (0.960)
  Pallas kernels: 45.1 us -> 43.5 us
    pallas_call x1, Pallas kernels: 45.1 us -> 43.5 us  [fused_on_device(): pl.pallas_call(functools.partial(unit_kernel, N, Q), out_shape=(jax.Shape...]
where the time goes in v4:
time: 50.2 us; the launch traced here: 49.9 us
  Pallas kernels  43.5 us (87%)
  local copies, waits for them, and re-layouts  5.12 us (10%)
  between operations  1.29 us (3%)
    pallas_call x1, Pallas kernels, fused_on_device(): pl.pallas_call(functools.partial(unit_kernel, N, Q), out_shape=(jax.Shape...  43.5 us
    unnamed x3, local copies, waits for them, and re-layouts  5.12 us

profile of v4, /device:TPU:0, one launch (start us, length us, event | category | flops | bytes accessed | tf_op | source)
XLA Modules:
  0.0 49.9 jit_solution(12291755917099171720)
XLA Ops:
  1.3 43.5 %shard_map.112 = (bf16[256,128]{1,0:T(8,128)(2,1)}, bf16[256,128]{1,0:T(8,128)(2,1)}, bf16[3456,128]{1,0:T(8,128)(2,1)}) custom-call(bf16[256,256]{1,0:T(8,128)(2,1)} %bitcast.6, s32[27,256]{1,0:T(8,128)} %nb_hbm.1, s32[4,32]{1,0:T(4,128)} %sr_hbm.1, s32[1]{0:T(128)S(6)} %copy.15.noise_ref, bf16[27,256,128]{2,1,0:T(8,128)(2,1)} %w_hbm.1, ...), custom_call_target="tpu_custom_call" | custom-call | tf_op jit(solution)/shard_map/pallas_call | solution.py:566
  44.8 1.5 %copy.16 = bf16[1,256,128]{2,1,0:T(8,128)(2,1)} copy(bf16[1,256,128]{2,1,0:T(8,128)(2,1)} %bitcast.9) | data formatting | bytes 131072
  46.3 1.5 %copy.17 = bf16[1,256,128]{2,1,0:T(8,128)(2,1)} copy(bf16[1,256,128]{2,1,0:T(8,128)(2,1)} %bitcast.8) | data formatting | bytes 131072
  47.8 2.2 %copy.18 = bf16[27,128,128]{2,1,0:T(8,128)(2,1)} copy(bf16[27,128,128]{2,1,0:T(8,128)(2,1)} %bitcast.5) | data formatting | bytes 1769472
